TPU v7x, 32 devices: a whole 2x2x4 slice. The times are simulated.
32 devices in a mesh: chan: 2 (over y), col: 4 (over x, core), row: 4 (over z).
Axes of the slice: x: 2, y: 2, z: 4, core: 2. Of those that a mesh axis runs over, the one named last changes fastest.
Arguments:
- visibilities: bfloat16 [2, 32768], P(None, ('chan', 'col', 'row')), parts along dimension 1, may hold values from -0.01171875 to 0.01171875
- taps: bfloat16 [2, 8, 32768], P(None, None, ('chan', 'col', 'row')), parts along dimension 2, may hold values from 0.049804688 to 1
- targets: int32 [32768, 1], P(('chan', 'col', 'row')), parts along dimension 0, may hold values from 0 to 15; in each aligned block of 1024 rows (0 to 1023, 1024 to 2047, ...) at most 192 rows name the same one
- offsets: int32 [2, 32768], P(None, ('chan', 'col', 'row')), parts along dimension 1, may hold values from 0 to 504
- corr_x: float32 [1536], P('col'), may hold values from 0.5 to 1.5
- corr_y: float32 [1536], P('row'), may hold values from 0.5 to 1.5
- windows: int32 [2, 2], replicated, may hold values from 0 to 31232
Outputs:
- facets: float32 [4, 2, 1536, 1536], P('chan', None, 'col', 'row'), parts along dimension 0
There are 2 independent parts, one for each index of `chan`. A program takes and returns all parts, laid end to end along the dimension named above; an argument that names none is the same for every part. Nothing has to cross between parts.
Inputs may be any that keep to these rules, and one draw needn't show every extreme that they name: `targets`: within the 1024 rows of one device, no subgrid is named by more than 192 rows, a bound that some block reaches.
All inputs are finite; a program needn't handle non-finite values.
Results may differ from a plain program's by a relative error of at most 0.015.
Values may be sent and summed in bfloat16 or wider, within the bound.
A program may use at most 64 MiB of HBM per device.

v0:
```python
import math

import jax
import jax.numpy as jnp
from jax import lax
from jax.sharding import PartitionSpec as P

IMAGE = 32768
SUBGRID = 512
FACET = 1536


def phase_table(first, second):
    product = jnp.mod(first[:, None] * second[None, :], IMAGE)
    angle = product.astype(jnp.float32) * (2.0 * math.pi / IMAGE)
    return (jnp.cos(angle).astype(jnp.bfloat16), jnp.sin(angle).astype(jnp.bfloat16))


def placed_kernel(kernel_taps, kernel_offsets):
    relative = jnp.arange(SUBGRID, dtype=jnp.int32)[None, :] - kernel_offsets[:, None]
    placed = jnp.zeros(relative.shape, jnp.bfloat16)
    for tap_index in range(kernel_taps.shape[0]):
        placed = jnp.where(relative == tap_index, kernel_taps[tap_index][:, None], placed)
    return placed


def grid_subgrid(values, kernel_taps, kernel_offsets):
    first_kernel = placed_kernel(kernel_taps[0], kernel_offsets[0])
    second_kernel = placed_kernel(kernel_taps[1], kernel_offsets[1])
    weighted = jnp.concatenate(
        [values[0][:, None] * second_kernel, values[1][:, None] * second_kernel], axis=1
    )
    gridded = lax.dot_general(
        first_kernel, weighted, (((0,), (0,)), ((), ())), preferred_element_type=jnp.float32
    )
    return gridded.astype(jnp.bfloat16)


def row_block(gridded, row_corner, windows, row_number):
    real_part = gridded[:, :SUBGRID].T
    imag_part = gridded[:, SUBGRID:].T
    stacked = jnp.concatenate(
        [jnp.concatenate([real_part, imag_part], 1), jnp.concatenate([-imag_part, real_part], 1)], 0
    )
    cell_ids = jnp.mod(row_corner + jnp.arange(SUBGRID, dtype=jnp.int32), IMAGE)
    pieces = []
    for facet_idx in range(windows.shape[0]):
        pixels = windows[facet_idx, 1] + jnp.arange(row_number, dtype=jnp.int32)
        cosine, sine_part = phase_table(pixels, cell_ids)
        tables = jnp.concatenate([cosine, sine_part], 1)
        pieces.append(jnp.dot(tables, stacked, preferred_element_type=jnp.float32))
    return jnp.concatenate(pieces, 1)


def column_block(column, col_corner, windows, row_number):
    cell_ids = jnp.mod(col_corner + jnp.arange(SUBGRID, dtype=jnp.int32), IMAGE)
    pieces = []
    for facet_idx in range(windows.shape[0]):
        facet_block = column[:, facet_idx * 2 * SUBGRID : (facet_idx + 1) * 2 * SUBGRID]
        real_part = facet_block[:, :SUBGRID].T
        imag_part = facet_block[:, SUBGRID:].T
        stacked = jnp.concatenate(
            [
                jnp.concatenate([real_part, imag_part], 1),
                jnp.concatenate([-imag_part, real_part], 1),
            ],
            0,
        )
        pixels = windows[facet_idx, 0] + jnp.arange(row_number, dtype=jnp.int32)
        cosine, sine_part = phase_table(pixels, cell_ids)
        tables = jnp.concatenate([cosine, sine_part], 1)
        pieces.append(jnp.dot(tables, stacked, preferred_element_type=jnp.float32))
    return jnp.concatenate(pieces, 1)


def body(visibilities, taps, targets, offsets, corr_x, corr_y, windows):
    column_total = lax.axis_size("col")
    row_devices = lax.axis_size("row")
    subgrids = column_total * row_devices
    row_total = targets.shape[0]
    capacity = 3 * row_total // subgrids
    slot_total = subgrids * capacity
    own_column = lax.axis_index("col")
    own_row = lax.axis_index("row")
    facet_count = windows.shape[0]
    tap_count = taps.shape[1]
    onehot = (targets == jnp.arange(subgrids, dtype=jnp.int32)[None, :]).astype(jnp.int32)
    running = jnp.cumsum(onehot, axis=0)
    position = jnp.sum(running * onehot, axis=1) - 1
    slot_index = targets[:, 0] * capacity + position
    payload = jnp.concatenate(
        [
            visibilities,
            taps[0],
            taps[1],
            (offsets // 32).astype(jnp.bfloat16),
            (offsets % 32).astype(jnp.bfloat16),
        ],
        0,
    )
    fields = payload.shape[0]
    outgoing = jnp.zeros((fields, slot_total), jnp.bfloat16).at[:, slot_index].set(payload)
    incoming = lax.all_to_all(outgoing, ("col", "row"), split_axis=1, concat_axis=1, tiled=True)
    rec_values = incoming[0:2]
    rec_taps = incoming[2 : 2 + 2 * tap_count].reshape(2, tap_count, slot_total)
    upper_part = incoming[2 + 2 * tap_count : 4 + 2 * tap_count].astype(jnp.float32)
    lower_part = incoming[4 + 2 * tap_count : 6 + 2 * tap_count].astype(jnp.float32)
    rec_offsets = (upper_part * 32.0 + lower_part).astype(jnp.int32)
    gridded = grid_subgrid(rec_values, rec_taps, rec_offsets)
    facet_rows = FACET // row_devices
    row_corner = jnp.mod((own_row - row_devices // 2) * SUBGRID, IMAGE)
    column_sum = lax.psum_scatter(
        row_block(gridded, row_corner, windows, lax.axis_size("row") * facet_rows).astype(
            jnp.bfloat16
        ),
        "row",
        scatter_dimension=0,
        tiled=True,
    )
    facet_cols = FACET // column_total
    col_corner = jnp.mod((own_column - column_total // 2) * SUBGRID, IMAGE)
    summed = lax.psum_scatter(
        column_block(column_sum, col_corner, windows, lax.axis_size("col") * facet_cols).astype(
            jnp.bfloat16
        ),
        "col",
        scatter_dimension=0,
        tiled=True,
    ).astype(jnp.float32)
    shaped = summed.reshape(facet_cols, facet_count, 2, facet_rows)
    scaled = shaped * corr_x[:, None, None, None] * corr_y[None, None, None, :]
    return jnp.transpose(scaled, (1, 2, 0, 3))


def solution(mesh):
    in_specs = (
        P(None, ("chan", "col", "row")),
        P(None, None, ("chan", "col", "row")),
        P(("chan", "col", "row"), None),
        P(None, ("chan", "col", "row")),
        P("col"),
        P("row"),
        P(),
    )
    out_specs = P("chan", None, "col", "row")
    return jax.shard_map(body, mesh=mesh, in_specs=in_specs, out_specs=out_specs, check_vma=False)
```

profile of v0, /device:TPU:0, one launch (start us, length us, event | category | flops | bytes accessed | tf_op | source)
XLA Modules:
  0.0 286.1 jit_solution(5879891622389064788)
XLA Ops:
  6.5 0.7 slice_bitcast_fusion.2
  7.3 0.7 fusion.103
  8.0 1.0 concatenate.55
  9.0 0.2 copy.19
  9.2 0.7 fusion.102
  9.9 4.5 %reduce-window.6 = s32[16,8,128]{2,1,0:T(8,128)S(1)} reduce-window(s32[16,8,128]{2,1,0:T(8,128)S(1)} %fusion.102, s32[]{:T(128)} %constant.107.clone.1), window={size=1x1x128 pad=0_0x0_0x127_0}, to_apply=%region_0.0 | reduce-window | flops 2080768 | bytes 131076 | tf_op jit(solution)/shard_map/reduce-window
  14.4 0.1 slice.202
  14.4 0.1 copy.17
  14.7 0.1 broadcast_add_fusion
  14.8 0.7 fusion.101
  15.5 0.7 compare_select_fusion
  16.2 3.4 %scatter_custom_fusion = bf16[22,3072]{0,1:T(8,128)(2,1)S(1)} fusion(s32[1024]{0:T(1024)S(1)} %bitcast.58, bf16[1024,22]{1,0:T(8,128)(2,1)S(1)} %copy.19, bf16[]{:T(256)} %constant.111.clone.1), kind=kCustom, calls=%fused_computation.136 | custom fusion | bytes 135170 | tf_op jit(solution)/shard_map/scatter | solution.py:102
  19.7 1.1 copy.20
  20.7 7.4 %all-to-all-start = ((bf16[22,16,192]{2,0,1:T(8,128)(2,1)}), bf16[22,16,192]{2,0,1:T(8,128)(2,1)S(1)}, u32[]{:S(2)}, u32[]{:S(2)}) async-start(bf16[22,16,192]{2,0,1:T(8,128)(2,1)} %copy.20), calls=%async_computation | async-start | bytes 393216 | tf_op jit(solution)/shard_map/all_to_all | solution.py:103
  28.2 0.7 fusion.123
  28.9 1.3 iota_add_fusion.1
  30.2 27.2 %cosine_convert_fusion.2 = (bf16[1536,512]{1,0:T(8,128)(2,1)}, bf16[1536,512]{1,0:T(8,128)(2,1)}, bf16[1536,512]{1,0:T(8,128)(2,1)S(1)}, bf16[1536,512]{1,0:T(8,128)(2,1)S(1)}) fusion(s32[512]{0:T(512)S(1)} %add_select_fusion.4, s32[1536]{0:T(1024)S(1)} %get-tuple-element.54, s32[1536]{0:T(1024)S(1)} %get-tuple-element.53), kind=kLoop, calls=%fused_computation.103 | loop fusion | flops 25165824 | bytes 6305792 | tf_op jit(solution)/shard_map/convert_element_type | solution.py:16
  57.5 0.6 slice_reduce_fusion.18
  58.1 0.1 broadcast_in_dim.149
  58.2 0.1 broadcast_in_dim.151
  58.3 0.1 broadcast_in_dim.153
  58.4 0.1 broadcast_in_dim.155
  58.4 0.1 broadcast_in_dim.157
  58.5 0.1 broadcast_in_dim.159
  58.6 0.1 broadcast_in_dim.161
  58.7 0.1 broadcast_in_dim.163
  58.8 0.1 mul.134
  58.9 0.1 mul.137
  59.0 0.1 slice_reduce_fusion.19
  59.1 0.1 sub.58
  59.2 0.1 broadcast_in_dim.133
  59.3 0.1 broadcast_in_dim.135
  59.4 0.1 broadcast_in_dim.137
  59.5 0.1 broadcast_in_dim.139
  59.6 0.1 broadcast_in_dim.141
  59.7 0.1 broadcast_in_dim.143
  59.7 0.1 broadcast_in_dim.145
  59.8 0.1 broadcast_in_dim.147
  60.0 6.5 %broadcast_multiply_fusion.1 = (bf16[3072,512]{1,0:T(8,128)(2,1)S(1)}, bf16[3072,512]{1,0:T(8,128)(2,1)S(1)}) fusion(bf16[3072]{0:T(1024)(128)(2,1)S(1)} %mul.134, bf16[3072]{0:T(1024)(128)(2,1)S(1)} %broadcast_in_dim.163, bf16[3072]{0:T(1024)(128)(2,1)S(1)} %broadcast_in_dim.161, bf16[3072]{0:T(1024)(128)(2,1)S(1)} %broadcast_in_dim.159, ...), kind=kLoop, calls=%fused_computation.123 | loop fusion | flops 37748736 | bytes 6365184 | tf_op jit(solution)/shard_map/mul | solution.py:31
  66.6 6.6 %fusion.93 = bf16[512,1024]{1,0:T(8,128)(2,1)S(1)} fusion(bf16[3072,512]{1,0:T(8,128)(2,1)S(1)} %get-tuple-element.32, bf16[3072,512]{1,0:T(8,128)(2,1)S(1)} %get-tuple-element.31, s32[3072]{0:T(1024)S(1)} %sub.54, bf16[3072]{0:T(1024)(128)(2,1)S(1)} %broadcast_in_dim.147, bf16[3072]{0:T(1024)(128)(2,1)S(1)} %broadcast_in_dim.145, ...), kind=kOutput, calls=%fused_computation.133 | convolution fusion | flops 3261071360 | bytes 7401472 | tf_op jit(solution)/shard_map/dot_general | solution.py:33
  73.2 0.1 slice_bitcast_fusion
  73.3 1.3 copy-done
  74.6 0.5 copy-done.1
  75.1 3.5 %convolution_convert_fusion.1 = bf16[1536,1024]{0,1:T(8,128)(2,1)S(1)} fusion(bf16[1536,512]{1,0:T(8,128)(2,1)S(1)} %copy-done.1, bf16[1536,512]{1,0:T(8,128)(2,1)S(1)} %copy-done, bf16[512,512]{0,1:T(8,128)(2,1)S(1)} %get-tuple-element.30, bf16[512,512]{0,1:T(8,128)(2,1)S(1)} %fusion.121, bf16[512,512]{0,1:T(8,128)(2,1)S(1)} %get-tuple-element.29), kind=kOutput, calls=%fused_computation.62 | convolution fusion | flops 3237478400 | bytes 7864320 | tf_op jit(solution)/shard_map/dot_general | solution.py:51
  78.5 3.4 %convolution_convert_fusion = bf16[1536,1024]{0,1:T(8,128)(2,1)S(1)} fusion(bf16[1536,512]{1,0:T(8,128)(2,1)S(1)} %get-tuple-element.47, bf16[1536,512]{1,0:T(8,128)(2,1)S(1)} %get-tuple-element.48, bf16[512,512]{0,1:T(8,128)(2,1)S(1)} %get-tuple-element.30, bf16[512,512]{0,1:T(8,128)(2,1)S(1)} %fusion.121, bf16[512,512]{0,1:T(8,128)(2,1)S(1)} %get-tuple-element.29), kind=kOutput, calls=%fused_computation.61 | convolution fusion | flops 3237478400 | bytes 7864320 | tf_op jit(solution)/shard_map/dot_general | solution.py:51
  82.0 3.1 %pad_maximum_fusion = bf16[1536,2048]{0,1:T(8,128)(2,1)} fusion(bf16[1536,1024]{0,1:T(8,128)(2,1)S(1)} %convolution_convert_fusion, bf16[1536,1024]{0,1:T(8,128)(2,1)S(1)} %convolution_convert_fusion.1), kind=kLoop, calls=%fused_computation.5 | loop fusion | flops 12582912 | bytes 12582912 | tf_op jit(solution)/shard_map/concatenate | solution.py:52
  85.0 8.7 %copy.22 = bf16[1536,2048]{1,0:T(8,128)(2,1)} copy(bf16[1536,2048]{0,1:T(8,128)(2,1)} %pad_maximum_fusion) | data formatting | bytes 12582912
  93.8 1.3 iota_add_fusion
  95.1 27.7 %cosine_convert_fusion.3 = (bf16[1536,512]{1,0:T(8,128)(2,1)}, bf16[1536,512]{1,0:T(8,128)(2,1)}, bf16[1536,512]{1,0:T(8,128)(2,1)S(1)}, bf16[1536,512]{1,0:T(8,128)(2,1)}) fusion(s32[512]{0:T(512)S(1)} %add_select_fusion.5, s32[1536]{0:T(1024)S(1)} %get-tuple-element.56, s32[1536]{0:T(1024)S(1)} %get-tuple-element.55), kind=kLoop, calls=%fused_computation.105 | loop fusion | flops 25165824 | bytes 6305792 | tf_op jit(solution)/shard_map/convert_element_type | solution.py:16
  122.8 83.2 %reduce-scatter.7.cloned.1.call-done = bf16[384,2048]{1,0:T(8,128)(2,1)} async-done(((bf16[1536,2048]{1,0:T(8,128)(2,1)}), bf16[384,2048]{1,0:T(8,128)(2,1)}) %reduce-scatter.7.cloned.1.call-update) | async-done | bytes 1572880
  206.0 1.5 fusion.122
  207.4 0.2 copy.27
  207.7 0.8 bitcast_negate_fusion.1
  208.5 0.9 copy.26
  209.4 0.2 copy.29
  209.7 0.2 copy.28
  209.9 5.0 %convolution_convert_fusion.3 = bf16[1536,768]{0,1:T(8,128)(2,1)S(1)} fusion(bf16[1536,512]{1,0:T(8,128)(2,1)} %get-tuple-element.36, bf16[1536,512]{1,0:T(8,128)(2,1)} %get-tuple-element.35, bf16[512,384]{1,0:T(8,128)(2,1)} %bitcast.51, bf16[512,384]{1,0:T(8,128)(2,1)} %bitcast_negate_fusion.1, bf16[512,384]{1,0:T(8,128)(2,1)S(1)} %bitcast.49), kind=kOutput, calls=%fused_computation.64 | convolution fusion | flops 2429681664 | bytes 6684672 | tf_op jit(solution)/shard_map/dot_general | solution.py:72
  214.9 2.7 convolution_convert_fusion.2
  217.5 2.5 pad_maximum_fusion.1
  220.0 6.6 %copy.24 = bf16[1536,1536]{1,0:T(8,128)(2,1)} copy(bf16[1536,1536]{0,1:T(8,128)(2,1)} %pad_maximum_fusion.1) | data formatting | bytes 9437184
  226.7 48.5 %reduce-scatter.9.cloned.1.call-done = bf16[384,1536]{1,0:T(8,128)(2,1)} async-done(((bf16[1536,1536]{1,0:T(8,128)(2,1)}), bf16[384,1536]{1,0:T(8,128)(2,1)}) %reduce-scatter.9.cloned.1.call-update) | async-done | bytes 1179664
  275.2 1.7 copy.25
  276.9 0.6 copy.21
  277.6 1.7 multiply_bitcast_fusion
  (25 shorter events, 0.5 us)
Async XLA Ops:
  6.5 21.7 %copy-start.3 = (s32[2,2]{1,0:T(2,128)S(1)}, s32[2,2]{1,0:T(2,128)}, u32[]{:S(2)}) copy-start(s32[2,2]{1,0:T(2,128)} %param.13) | copy-start | bytes 52
  20.7 36.7 %all-to-all-start = ((bf16[22,16,192]{2,0,1:T(8,128)(2,1)}), bf16[22,16,192]{2,0,1:T(8,128)(2,1)S(1)}, u32[]{:S(2)}, u32[]{:S(2)}) async-start(bf16[22,16,192]{2,0,1:T(8,128)(2,1)} %copy.20), calls=%async_computation | async-start | bytes 393216 | tf_op jit(solution)/shard_map/all_to_all | solution.py:103
  28.1 177.9 %reduce-scatter.7.cloned.1.call-start = ((), (), s32[]{:S(2)}) async-start(), calls=%async_computation.3 | async-start | bytes 7864320
  73.2 1.4 copy-start
  73.2 1.9 copy-start.1
  93.7 181.5 %reduce-scatter.9.cloned.1.call-start = ((), (), s32[]{:S(2)}) async-start(), calls=%async_computation.4 | async-start | bytes 5898240
  209.9 5.0 %copy-start.2 = (bf16[1536,512]{1,0:T(8,128)(2,1)S(1)}, bf16[1536,512]{1,0:T(8,128)(2,1)}, u32[]{:S(2)}) copy-start(bf16[1536,512]{1,0:T(8,128)(2,1)} %get-tuple-element.46) | copy-start | bytes 4718596
  226.7 50.9 %copy-start.4 = (f32[384]{0:T(512)S(1)}, f32[384]{0:T(512)}, u32[]{:S(2)}) copy-start(f32[384]{0:T(512)} %param.12) | copy-start | bytes 4612
  226.7 50.9 %copy-start.5 = (f32[384]{0:T(512)S(1)}, f32[384]{0:T(512)}, u32[]{:S(2)}) copy-start(f32[384]{0:T(512)} %param.11) | copy-start | bytes 4612
Sparse Core Ops, SparseCore 0:
  93.9 112.0 reduce-scatter.6
  226.8 48.3 reduce-scatter.8
where the time goes:
time: 287 us; the launch traced here: 286 us
  waiting for transfers between devices  132 us (46%)
  other arithmetic  79.7 us (28%)
  local copies, waits for them, and re-layouts  32.3 us (11%)
  matrix products  21.1 us (7%)
  between operations  13.7 us (5%)
  starting transfers between devices  7.44 us (3%)
    unnamed x4, waiting for transfers between devices  132 us
    convert_element_type x2, other arithmetic, phase_table(): jnp.cos(angle).astype(jnp.bfloat16)  54.9 us
    unnamed x19, local copies, waits for them, and re-layouts  20.3 us
    dot_general x2, matrix products, column_block(): pieces.append(jnp.dot(tables, stacked, preferred_element_type=jnp.float32))  7.61 us
    all_to_all x1, starting transfers between devices, body(): lax.all_to_all(outgoing, ('col', 'row'), split_axis=1, concat_axis=1, til...  7.36 us
    dot_general x2, matrix products, row_block(): pieces.append(jnp.dot(tables, stacked, preferred_element_type=jnp.float32))  6.9 us
    dot_general x1, matrix products, grid_subgrid(): lax.dot_general(first_kernel, weighted, (((0,), (0,)), ((), ())), preferr...  6.61 us
    mul x1, other arithmetic, grid_subgrid(): values[0][:, None] * second_kernel  6.55 us
  transfers between devices with their start and end apart: 3, of which 2 were waited for; matrix products, arithmetic and copies ran while one was open for 20% of the time, Pallas kernels for 0%

commit v1 on v0

v1 whole, which is shorter than its diff:
```python
import functools
import math

import jax
import jax.numpy as jnp
from jax import lax
from jax.experimental import pallas as pl
from jax.experimental.pallas import tpu as pltpu
from jax.sharding import PartitionSpec as P

IMAGE = 32768
SUBGRID = 512
FACET = 1536
UNIT = 16
CHUNK = 256
FIELDS = 32
STEP = 32
F32 = jnp.float32
BF16 = jnp.bfloat16
NT = (((1,), (1,)), ((), ()))


def sincos(product):
    angle = jnp.mod(product, IMAGE).astype(F32) * (2.0 * math.pi / IMAGE)
    return jnp.cos(angle), jnp.sin(angle)


def split_table(start, count, other):
    coarse = jnp.mod(start + STEP * jnp.arange(count // STEP, dtype=jnp.int32), IMAGE)
    fine = jnp.arange(STEP, dtype=jnp.int32)
    cos_a, sin_a = sincos(coarse[:, None] * other[None, :])
    cos_b, sin_b = sincos(fine[:, None] * other[None, :])
    cos_a, sin_a = cos_a[:, None], sin_a[:, None]
    cosine = (cos_a * cos_b - sin_a * sin_b).astype(BF16).reshape(count, -1)
    sine = (sin_a * cos_b + cos_a * sin_b).astype(BF16).reshape(count, -1)
    return cosine, sine


def pack_kernel(quarter, vis_ref, taps_ref, targets_ref, offsets_ref, out_ref):
    rows = vis_ref.shape[1]
    targets = targets_ref[...]
    named = lax.broadcasted_iota(jnp.int32, (128, rows), 0) == targets
    onehot = jnp.where(named, 1.0, 0.0)
    onehot16 = onehot.astype(BF16)
    counts = lax.dot_general(jnp.ones((16, rows), BF16), onehot16, NT, preferred_element_type=F32)
    units = jnp.floor((counts + (UNIT - 1.0)) * (1.0 / UNIT))
    before = lax.broadcasted_iota(jnp.int32, (128, 128), 0) < lax.broadcasted_iota(
        jnp.int32, (128, 128), 1
    )
    starts = jnp.dot(
        units.astype(BF16), jnp.where(before, 1.0, 0.0).astype(BF16), preferred_element_type=F32
    )
    upto = lax.broadcasted_iota(jnp.int32, (rows, rows), 0) <= lax.broadcasted_iota(
        jnp.int32, (rows, rows), 1
    )
    running = jnp.dot(
        onehot16, jnp.where(upto, 1.0, 0.0).astype(BF16), preferred_element_type=F32
    )
    rank = jnp.sum(running * onehot, axis=0, keepdims=True) - 1.0
    first = jnp.dot(starts.astype(BF16), onehot16, preferred_element_type=F32)[0:1]
    slot = (first * UNIT + rank).astype(jnp.int32)

    lane_pos = lax.broadcasted_iota(jnp.int32, (8, rows), 0)
    placed = []
    for dim in range(2):
        wanted = (lane_pos - offsets_ref[dim : dim + 1, :]) & 7
        value = jnp.zeros((8, rows), F32)
        for tap in range(8):
            row = taps_ref[dim * 8 + tap : dim * 8 + tap + 1, :].astype(F32)
            value = jnp.where(wanted == tap, row, value)
        placed.append(value)
    vis = vis_ref[...].astype(F32)
    offsets = offsets_ref[...]
    upper = (offsets >> 3).astype(F32)
    lower = (offsets & 7).astype(F32)
    extra = jnp.zeros((8, rows), F32)
    for idx, row in enumerate((upper[0:1], lower[0:1], upper[1:2], lower[1:2])):
        extra = jnp.where(lane_pos == idx, row, extra)
    fields = jnp.concatenate(
        [placed[0], placed[1] * vis[0:1], placed[1] * vis[1:2], extra], 0
    ).astype(BF16)
    blank = jnp.zeros_like(fields)
    total = jnp.zeros((quarter, 128), F32)
    slot_ids = lax.broadcasted_iota(jnp.int32, (quarter, rows), 0)
    for part in range(4):
        chosen = jnp.where(slot_ids == slot - part * quarter, 1.0, 0.0).astype(BF16)
        spread = jnp.concatenate([fields if b == part else blank for b in range(4)], 0)
        total += lax.dot_general(chosen, spread, NT, preferred_element_type=F32)
    out_ref[0:quarter, :] = total.astype(BF16)
    which = lax.broadcasted_iota(jnp.int32, (16, 128), 0)
    out_ref[quarter:, :] = jnp.where(
        which == 0, starts, jnp.where(which == 1, units, 0.0)
    ).astype(BF16)


def grid_kernel(
    sources, row_devices, quarter, block, facets,
    starts_ref, units_ref, rows_ref, table_ref, out_ref, packed, grid_sum, sums,
):
    col, row = pl.program_id(0), pl.program_id(1)
    subgrid = col * row_devices + row
    subs = pl.num_programs(0) * row_devices
    per_quarter = quarter // UNIT
    lane_block = lax.broadcasted_iota(jnp.int32, (UNIT, 128), 1) // FIELDS

    def gather(source, pos):
        start = starts_ref[source * subs + subgrid]
        count = units_ref[source * subs + subgrid]

        def four(step, carry):
            for inner in range(4):
                unit = start + step * 4 + inner
                part = unit // per_quarter
                place = pl.multiple_of((unit - part * per_quarter) * UNIT, UNIT)
                data = rows_ref[source, pl.ds(place, UNIT), :]
                data = jnp.where(lane_block == part, data.astype(F32), 0.0).astype(BF16)
                to = pl.multiple_of((pos + step * 4 + inner) * UNIT, UNIT)
                packed[pl.ds(to, UNIT), :] = data
            return carry

        lax.fori_loop(0, (count + 3) // 4, four, 0)
        return pos + count

    total = lax.fori_loop(0, sources, gather, 0)
    packed[pl.ds(pl.multiple_of(total * UNIT, UNIT), CHUNK), :] = jnp.zeros((CHUNK, 128), BF16)
    grid_sum[...] = jnp.zeros_like(grid_sum)

    out_row = lax.broadcasted_iota(jnp.int32, (64, 128), 0)
    lane = lax.broadcasted_iota(jnp.int32, (64, 128), 1) % FIELDS
    source_field = jnp.where(out_row < 24, out_row, 24 + (out_row - 24) // 8)
    pick = jnp.where((source_field == lane) & (out_row < 56), 1.0, 0.0).astype(BF16)
    cell = lax.broadcasted_iota(jnp.int32, (8, CHUNK), 0).astype(F32)

    def chunk(step, carry):
        data = packed[pl.ds(pl.multiple_of(step * CHUNK, CHUNK), CHUNK), :]
        field = lax.dot_general(pick, data, NT, preferred_element_type=F32)
        group_u = field[24:32] + jnp.where(cell < field[32:40], 1.0, 0.0)
        group_v = field[40:48] + jnp.where(cell < field[48:56], 1.0, 0.0)
        val_u, val_r, val_i = field[0:8], field[8:16], field[16:24]
        kern_u, kern_r, kern_i = [], [], []
        for g in range(SUBGRID // 8):
            hit_v = group_v == float(g)
            kern_u.append(jnp.where(group_u == float(g), val_u, 0.0))
            kern_r.append(jnp.where(hit_v, val_r, 0.0))
            kern_i.append(jnp.where(hit_v, val_i, 0.0))
        left = jnp.concatenate(kern_u, 0).astype(BF16)
        right = jnp.concatenate(kern_r + kern_i, 0).astype(BF16)
        grid_sum[...] += lax.dot_general(left, right, NT, preferred_element_type=F32)
        return carry

    lax.fori_loop(0, (total * UNIT + CHUNK - 1) // CHUNK, chunk, 0)

    @pl.when(row == 0)
    def _():
        sums[...] = jnp.zeros_like(sums)

    table = table_ref[...]
    real = jnp.dot(grid_sum[:, :SUBGRID].astype(BF16), table, preferred_element_type=F32)
    imag = jnp.dot(grid_sum[:, SUBGRID:].astype(BF16), table, preferred_element_type=F32)
    for f in range(facets):
        lo, mid, hi = 2 * f * block, (2 * f + 1) * block, (2 * f + 2) * block
        sums[:, lo:mid] += real[:, lo:mid] - imag[:, mid:hi]
        sums[:, mid:hi] += real[:, mid:hi] + imag[:, lo:mid]

    @pl.when(row == row_devices - 1)
    def _():
        for f in range(facets):
            out_ref[f] = sums[:, 2 * f * block : 2 * (f + 1) * block].astype(BF16)


def column_kernel(block, cos_ref, sin_ref, part_ref, out_ref):
    value = part_ref[0]
    first = jnp.dot(cos_ref[0, 0], value, preferred_element_type=F32)
    second = jnp.dot(sin_ref[0, 0], value, preferred_element_type=F32)
    out_ref[0, 0, 0] = (first[:, :block] - second[:, block:]).astype(BF16)
    out_ref[0, 0, 1] = (first[:, block:] + second[:, :block]).astype(BF16)


def body(visibilities, taps, targets, offsets, corr_x, corr_y, windows):
    cols = lax.axis_size("col")
    row_devices = lax.axis_size("row")
    subgrids = cols * row_devices
    sources = subgrids
    rows = targets.shape[0]
    cap = 3 * rows // subgrids
    half = cols // 2
    own_col = lax.axis_index("col")
    own_row = lax.axis_index("row")
    core = lax.rem(own_col, 2)
    facets = windows.shape[0]
    block = FACET // row_devices
    pix_rows = FACET // cols
    quarter = -(-(rows + subgrids * (UNIT - 1)) // (4 * UNIT)) * UNIT

    packed = pl.pallas_call(
        functools.partial(pack_kernel, quarter),
        out_shape=jax.ShapeDtypeStruct((quarter + 16, 128), BF16),
        compiler_params=pltpu.CompilerParams(vmem_limit_bytes=40 << 20),
        name="pack_rows",
    )(visibilities, taps.reshape(-1, rows), targets.reshape(1, rows), offsets)
    gathered = lax.all_gather(packed, ("col", "row"), axis=0, tiled=False)

    cells = jnp.int32(IMAGE - row_devices // 2 * SUBGRID)
    pieces = []
    for f in range(facets):
        pixels = windows[f, 1] + own_row * block + jnp.arange(block, dtype=jnp.int32)
        pieces += list(split_table(cells, row_devices * SUBGRID, pixels))
    row_table = jnp.concatenate(pieces, 1)
    first_cell = (core * half - cols // 2) * SUBGRID
    col_cells = jnp.mod(first_cell + jnp.arange(half * SUBGRID, dtype=jnp.int32), IMAGE)
    cosines, sines = [], []
    for f in range(facets):
        for who in (own_col + 1 - 2 * core, own_col):
            cosine, sine = split_table(windows[f, 0] + who * pix_rows, pix_rows, col_cells)
            cosines.append(cosine)
            sines.append(sine)
    col_cos = jnp.stack(cosines).reshape(facets, 2, pix_rows, half * SUBGRID)
    col_sin = jnp.stack(sines).reshape(facets, 2, pix_rows, half * SUBGRID)

    own_subs = half * row_devices
    meta = gathered[:, quarter : quarter + 2, :].astype(jnp.int32)
    meta = lax.dynamic_slice(meta, (0, 0, core * own_subs), (sources, 2, own_subs))
    starts = meta[:, 0].reshape(-1)
    units = meta[:, 1].reshape(-1)
    room = sources * (-(-cap // UNIT)) * UNIT + CHUNK + 4 * UNIT
    width = facets * 2 * block
    parts = pl.pallas_call(
        functools.partial(grid_kernel, sources, row_devices, quarter, block, facets),
        grid_spec=pltpu.PrefetchScalarGridSpec(
            num_scalar_prefetch=2,
            grid=(half, row_devices),
            in_specs=[
                pl.BlockSpec(
                    (sources, quarter + 16, 128),
                    lambda c, r, *_: (0, 0, 0),
                    pipeline_mode=pl.Buffered(1),
                ),
                pl.BlockSpec((SUBGRID, width), lambda c, r, *_: (r, 0)),
            ],
            out_specs=pl.BlockSpec((facets, SUBGRID, 2 * block), lambda c, r, *_: (0, c, 0)),
            scratch_shapes=[
                pltpu.VMEM((room, 128), BF16),
                pltpu.VMEM((SUBGRID, 2 * SUBGRID), F32),
                pltpu.VMEM((SUBGRID, width), F32),
            ],
        ),
        out_shape=jax.ShapeDtypeStruct((facets, half * SUBGRID, 2 * block), BF16),
        compiler_params=pltpu.CompilerParams(vmem_limit_bytes=56 << 20),
        name="grid_rows",
    )(starts, units, gathered, row_table)

    depth = half * SUBGRID
    table_spec = pl.BlockSpec((1, 1, pix_rows, depth), lambda w, f: (f, w, 0, 0))
    images = pl.pallas_call(
        functools.partial(column_kernel, block),
        grid=(2, facets),
        in_specs=[
            table_spec,
            table_spec,
            pl.BlockSpec((1, depth, 2 * block), lambda w, f: (f, 0, 0)),
        ],
        out_specs=pl.BlockSpec((1, 1, 2, pix_rows, block), lambda w, f: (w, f, 0, 0, 0)),
        out_shape=jax.ShapeDtypeStruct((2, facets, 2, pix_rows, block), BF16),
        compiler_params=pltpu.CompilerParams(vmem_limit_bytes=56 << 20),
        name="column_sums",
    )(col_cos, col_sin, parts)
    swap = [(c, c ^ 1) for c in range(cols)]
    other = lax.ppermute(images[0], "col", swap)
    summed = images[1].astype(F32) + other.astype(F32)
    return summed * corr_x[None, None, :, None] * corr_y[None, None, None, :]


def solution(mesh):
    in_specs = (
        P(None, ("chan", "col", "row")),
        P(None, None, ("chan", "col", "row")),
        P(("chan", "col", "row"), None),
        P(None, ("chan", "col", "row")),
        P("col"),
        P("row"),
        P(),
    )
    out_specs = P("chan", None, "col", "row")
    return jax.shard_map(body, mesh=mesh, in_specs=in_specs, out_specs=out_specs, check_vma=False)
```

time: 287 us -> 140 us (0.49)
  waiting for transfers between devices: 132 us -> 25.1 us
  Pallas kernels: 0 us -> 72 us
  other arithmetic: 79.7 us -> 16.2 us
  local copies, waits for them, and re-layouts: 32.3 us -> 7.85 us
  matrix products: 21.1 us -> 0 us
  starting transfers between devices: 7.44 us -> 0.07 us
  between operations: 13.7 us -> 17.3 us
    unnamed x4 -> x1, waiting for transfers between devices: 132 us -> 0.02 us
    pallas_call x0 -> x3, Pallas kernels: none -> 72 us  [the longest x1 60.6 us: body(): pl.pallas_call(functools.partial(grid_kernel, sources, row_devices, quart...]
    convert_element_type x5 -> x3, other arithmetic: 56.4 us -> 4.49 us  [the longest x1 2.35 us: split_table(): sine = (sin_a * cos_b + cos_a * sin_b).astype(BF16).reshape(count, -1)]
    all_gather x0 -> x1, waiting for transfers between devices: none -> 22.2 us  [body(): gathered = lax.all_gather(packed, ('col', 'row'), axis=0, tiled=False)]
    dot_general x5 -> x0, matrix products: 21.1 us -> none  [the longest x2 7.61 us: column_block(): pieces.append(jnp.dot(tables, stacked, preferred_element_type=jnp.float32))]
    unnamed x19 -> x14, local copies, waits for them, and re-layouts: 20.3 us -> 2.84 us
    all_to_all x1 -> x0, starting transfers between devices: 7.36 us -> none  [body(): lax.all_to_all(outgoing, ('col', 'row'), split_axis=1, concat_axis=1, til...]
    mul x1, other arithmetic: 6.55 us -> 1.81 us  [body(): return summed * corr_x[None, None, :, None] * corr_y[None, None, None, :]]
  transfers between devices with their start and end apart: 3 -> 2, of which waited for: 2 -> 2; matrix products, arithmetic and copies ran while one was open for 20% -> 11% of each run, Pallas kernels for 0% -> 0%
where the time goes in v1:
time: 140 us; the launch traced here: 138 us
  Pallas kernels  72 us (51%)
  waiting for transfers between devices  25.1 us (18%)
  between operations  17.3 us (12%)
  other arithmetic  16.2 us (12%)
  local copies, waits for them, and re-layouts  7.85 us (6%)
    pallas_call x1, Pallas kernels, body(): pl.pallas_call(functools.partial(grid_kernel, sources, row_devices, quart...  60.6 us
    all_gather x1, waiting for transfers between devices, body(): gathered = lax.all_gather(packed, ('col', 'row'), axis=0, tiled=False)  22.2 us
    pallas_call x1, Pallas kernels, body(): pl.pallas_call(functools.partial(column_kernel, block), grid=(2, facets),...  9.19 us
    concatenate x1, other arithmetic, body(): row_table = jnp.concatenate(pieces, 1)  3.16 us
    cos x5, other arithmetic, sincos(): return (jnp.cos(angle), jnp.sin(angle))  2.9 us
    unnamed x14, local copies, waits for them, and re-layouts  2.84 us
    ppermute x1, waiting for transfers between devices, body(): other = lax.ppermute(images[0], 'col', swap)  2.83 us
  transfers between devices with their start and end apart: 2, of which 2 were waited for; matrix products, arithmetic and copies ran while one was open for 11% of the time, Pallas kernels for 0%

profile of v1, /device:TPU:0, one launch (start us, length us, event | category | flops | bytes accessed | tf_op | source)
XLA Modules:
  0.0 138.5 jit_solution(275109686127446875)
XLA Ops:
  6.5 0.0 all-gather.3.cloned.1.call-start
  6.5 0.0 copy-start
  6.5 0.8 copy-done
  7.3 0.0 copy-start.1
  7.3 0.7 copy-done.1
  8.0 0.0 copy-start.2
  8.0 0.7 copy-done.2
  8.7 0.0 copy-start.3
  8.7 0.7 copy-done.3
  9.4 2.2 %pack_rows.1 = bf16[336,128]{1,0:T(8,128)(2,1)} custom-call(bf16[2,1024]{1,0:T(2,128)(2,1)S(1)} %copy-done.2, bf16[16,1024]{1,0:T(8,128)(2,1)S(1)} %bitcast.28, s32[1,1024]{1,0:T(1,128)S(1)} %bitcast.29, s32[2,1024]{1,0:T(2,128)S(1)} %copy-done.1), custom_call_target="tpu_custom_call" | custom-call | tf_op jit(solution)/shard_map/pack_rows/pallas_call | solution.py:195
  11.6 0.0 all-gather.3.cloned.1.call-update
  11.6 1.5 %fusion.65 = (s32[1,1]{1,0:T(1,128)}, s32[1,1]{1,0:T(1,128)}, s32[1,1]{1,0:T(1,128)}, s32[1,1]{1,0:T(1,128)}) fusion(s32[2,2]{1,0:T(2,128)} %param.13), kind=kLoop, calls=%fused_computation.146 | loop fusion | bytes 32 | tf_op jit(solution)/shard_map/slice | solution.py:206
  14.5 0.2 fusion.55
  14.7 0.2 fusion.53
  14.9 0.8 fusion.41
  16.8 0.5 fusion.27
  18.8 1.1 fusion.51
  19.9 2.3 %add_convert_fusion.5 = (bf16[12,32,1024]{2,1,0:T(8,128)(2,1)S(1)}, bf16[12,32,1024]{2,1,0:T(8,128)(2,1)S(1)}, bf16[12,32,1024]{2,1,0:T(8,128)(2,1)S(1)}, bf16[1...) fusion(f32[32,1024]{1,0:T(8,128)S(1)} %get-tuple-element.40, ...), kind=kLoop, calls=%fused_computation.13 | loop fusion | flops 12582912 | bytes 6946816 | tf_op jit(solution)/shard_map/convert_element_type | solution.py:35
  22.3 1.9 %pad_maximum_fusion.2 = bf16[4,384,1024]{2,1,0:T(8,128)(2,1)} fusion(bf16[1,384,1024]{2,1,0:T(8,128)(2,1)S(1)} %bitcast.43, bf16[1,384,1024]{2,1,0:T(8,128)(2,1)S(1)} %bitcast.42, bf16[1,384,1024]{2,1,0:T(8,128)(2,1)S(1)} %bitcast.41, bf16[1,384,1024]{2,1,0:T(8,128)(2,1)S(1)} %bitcast.40), kind=kLoop, calls=%fused_computation.2 | loop fusion | flops 4718592 | bytes 6291456 | tf_op jit(solution)/shard_map/stack | solution.py:218
  24.1 1.9 %pad_maximum_fusion.1 = bf16[4,384,1024]{2,1,0:T(8,128)(2,1)} fusion(bf16[1,384,1024]{2,1,0:T(8,128)(2,1)S(1)} %bitcast.39, bf16[1,384,1024]{2,1,0:T(8,128)(2,1)S(1)} %bitcast.38, bf16[1,384,1024]{2,1,0:T(8,128)(2,1)S(1)} %bitcast.37, bf16[1,384,1024]{2,1,0:T(8,128)(2,1)S(1)} %bitcast.36), kind=kLoop, calls=%fused_computation.1 | loop fusion | flops 4718592 | bytes 6291456 | tf_op jit(solution)/shard_map/stack | solution.py:217
  26.0 2.1 %subtract_convert_fusion = (bf16[64,32,384]{2,1,0:T(8,128)(2,1)S(1)}, bf16[64,32,384]{2,1,0:T(8,128)(2,1)S(1)}, bf16[64,32,384]{2,1,0:T(8,128)(2,1)S(1)}, bf16[64,32,384]{2,1,0:T(8,128)(2,1)S(1)}) fusion(f32[32,384]{1,0:T(8,128)S(1)} %get-tuple-element.48, f32[64,384]{1,0:T(8,128)S(1)} %get-tuple-element.53, f32[32,384]{1,0:T(8,128)S(1)} %get-tuple-element.47, ...), kind=kLoop, calls=%fused_computation.4 | loop fusion | flops 12582912 | bytes 6881280 | tf_op jit(solution)/shard_map/convert_element_type | solution.py:34
  28.1 3.2 %pad_maximum_fusion.table_ref = bf16[2048,1536]{1,0:T(8,128)(2,1)} fusion(bf16[2048,384]{1,0:T(8,128)(2,1)S(1)} %bitcast.33, bf16[2048,384]{1,0:T(8,128)(2,1)S(1)} %bitcast.32, bf16[2048,384]{1,0:T(8,128)(2,1)S(1)} %bitcast.34, bf16[2048,384]{1,0:T(8,128)(2,1)S(1)} %bitcast.35), kind=kLoop, calls=%fused_computation | loop fusion | flops 25165824 | bytes 12582912 | tf_op jit(solution)/shard_map/concatenate | solution.py:208
  31.2 22.2 %all-gather.3.cloned.1.call-done = bf16[5376,128]{1,0:T(8,128)(2,1)} async-done(((bf16[336,128]{1,0:T(8,128)(2,1)}), bf16[5376,128]{1,0:T(8,128)(2,1)}) %all-gather.3.cloned.1.call-update) | async-done | bytes 1376272 | tf_op jit(solution)/shard_map/all_gather | solution.py:201
  53.5 0.8 slice.38
  54.2 0.1 dynamic-slice_convert_fusion
  54.4 0.6 reshape_squeeze.6.starts_ref
  55.0 0.6 reshape_squeeze.7.units_ref
  55.5 60.6 %grid_rows.1.part_ref = bf16[2,1024,768]{2,1,0:T(8,128)(2,1)} custom-call(s32[128]{0:T(128)} %reshape_squeeze.6.starts_ref, s32[128]{0:T(128)} %reshape_squeeze.7.units_ref, bf16[16,336,128]{2,1,0:T(8,128)(2,1)} %bitcast.45, bf16[2048,1536]{1,0:T(8,128)(2,1)} %pad_maximum_fusion.table_ref), custom_call_target="tpu_custom_call" | custom-call | tf_op jit(solution)/shard_map/grid_rows/pallas_call | solution.py:227
  116.1 0.0 copy-start.5
  116.1 0.0 copy-start.6
  116.1 9.2 %column_sums.1 = bf16[2,2,2,384,384]{4,3,2,1,0:T(8,128)(2,1)} custom-call(bf16[2,2,384,1024]{3,2,1,0:T(8,128)(2,1)} %bitcast.31, bf16[2,2,384,1024]{3,2,1,0:T(8,128)(2,1)} %bitcast.30, bf16[2,1024,768]{2,1,0:T(8,128)(2,1)} %grid_rows.1.part_ref), custom_call_target="tpu_custom_call" | custom-call | tf_op jit(solution)/shard_map/column_sums/pallas_call | solution.py:254
  125.3 0.0 copy-start.4
  125.3 1.5 %slice_bitcast_fusion = bf16[2,2,384,384]{3,2,1,0:T(8,128)(2,1)S(1)} fusion(bf16[2,2,2,384,384]{4,3,2,1,0:T(8,128)(2,1)} %column_sums.1), kind=kLoop, calls=%fused_computation.18 | loop fusion | bytes 2359296 | tf_op jit(solution)/shard_map/squeeze | solution.py:268
  126.9 0.1 collective-permute-start
  127.0 2.8 %collective-permute-done = bf16[2,2,384,384]{3,2,1,0:T(8,128)(2,1)S(1)} collective-permute-done((bf16[2,2,384,384]{3,2,1,0:T(8,128)(2,1)S(1)}, bf16[2,2,384,384]{3,2,1,0:T(8,128)(2,1)S(1)}, u32[]{:S(2)}, u32[]{:S(2)}) %collective-permute-start) | collective-permute-done | bytes 1179680 | tf_op jit(solution)/shard_map/ppermute | solution.py:268
  129.8 0.0 copy-done.5
  129.8 0.0 copy-done.6
  129.8 0.0 copy-done.4
  129.8 1.8 %fusion.1 = f32[2,2,384,384]{3,2,1,0:T(8,128)} fusion(bf16[2,2,384,384]{3,2,1,0:T(8,128)(2,1)S(1)} %collective-permute-done, bf16[2,2,2,384,384]{4,3,2,1,0:T(8,128)(2,1)S(1)} %copy-done.4, f32[384]{0:T(512)S(1)} %copy-done.5, f32[384]{0:T(512)S(1)} %copy-done.6), kind=kLoop, calls=%fused_computation.9 | loop fusion | flops 2949120 | bytes 4721664 | tf_op jit(solution)/shard_map/mul | solution.py:270
  (7 shorter events, 0.1 us)
Async XLA Ops:
  6.5 46.9 %all-gather.3.cloned.1.call-start = ((), (), s32[]{:S(2)}) async-start(), calls=%async_computation | async-start | bytes 1462272 | tf_op jit(solution)/shard_map/all_gather | solution.py:201
  6.5 0.8 copy-start
  7.3 0.7 copy-start.1
  8.0 0.7 copy-start.2
  8.7 0.7 copy-start.3
  116.1 13.7 %copy-start.5 = (f32[384]{0:T(512)S(1)}, f32[384]{0:T(512)}, u32[]{:S(2)}) copy-start(f32[384]{0:T(512)} %param.12) | copy-start | bytes 4612
  116.1 13.7 %copy-start.6 = (f32[384]{0:T(512)S(1)}, f32[384]{0:T(512)}, u32[]{:S(2)}) copy-start(f32[384]{0:T(512)} %param.11) | copy-start | bytes 4612
  125.3 4.5 %copy-start.4 = (bf16[2,2,2,384,384]{4,3,2,1,0:T(8,128)(2,1)S(1)}, bf16[2,2,2,384,384]{4,3,2,1,0:T(8,128)(2,1)}, u32[]{:S(2)}) copy-start(bf16[2,2,2,384,384]{4,3,2,1,0:T(8,128)(2,1)} %column_sums.1) | copy-start | bytes 7077892
  126.9 2.9 %collective-permute-start = (bf16[2,2,384,384]{3,2,1,0:T(8,128)(2,1)S(1)}, bf16[2,2,384,384]{3,2,1,0:T(8,128)(2,1)S(1)}, u32[]{:S(2)}, u32[]{:S(2)}) collective-permute-start(bf16[2,2,384,384]{3,2,1,0:T(8,128)(2,1)S(1)} %slice_bitcast_fusion), channel_id=1, source_target_pairs={{0,4},{4,0},{8,12},{12,8},{1,5},{5,1},{9,13},{13,9},{2,6},{6,2},{1... | collective-permute-start | bytes 3538952 | tf_op jit(solution)/shard_map/ppermute | solution.py:268
Sparse Core Ops, SparseCore 0:
  11.7 41.7 all-gather.2
